TPU v7x, 512 devices: a whole 4x8x8 slice. The times are simulated.
512 devices in a mesh: cuts: 8 (over x, core), rows: 64 (over z, y).
Axes of the slice: x: 4, y: 8, z: 8, core: 2. Of those that a mesh axis runs over, the one named last changes fastest.
Arguments:
- start_modes: float32 [8, 256, 512, 128], P('cuts', 'rows'), may hold values from -6 to 6
- contrast: float32 [8, 256, 512], P('cuts', 'rows'), may hold values from 0 to 1
- rotations: float32 [8, 2, 128, 128], P('cuts'), may hold values from -0.2 to 1.2, as said below
- ordering: int32 [8, 2, 128], P('cuts'), may hold values from 0 to 127, each once within a row
Outputs:
- modes: float32 [8, 256, 512, 128], P('cuts', 'rows')
- coupling: float32 [8, 128, 128], P('cuts', 'rows')
- rayleigh: float32 [8, 128, 128], P('cuts', 'rows')
Inputs may be any that keep to these rules, and one draw needn't show every extreme that they name: `rotations`: each matrix is invertible.
All inputs are finite; a program needn't handle non-finite values.
Results may differ from a plain program's by a relative error of at most 0.00026.
Values sent between devices are 32-bit elements; how exact they have to be, the bound alone decides.
A program may use at most 64 MiB of HBM per device.

v0:
```python
import jax
import jax.numpy as jnp
from jax import lax
from jax.sharding import PartitionSpec as P

DEGREE = 4
ITERS = 2


def padded_2(block, sides, width):
    for axis, dim in sides:
        count = lax.axis_size(axis)
        forward = [(i, i + 1) for i in range(count - 1)]
        backward = [(target, source) for source, target in forward]
        low = lax.ppermute(
            lax.slice_in_dim(block, block.shape[dim] - width, None, axis=dim), axis, forward
        )
        high = lax.ppermute(lax.slice_in_dim(block, 0, width, axis=dim), axis, backward)
        block = jnp.concatenate([low, block, high], axis=dim)
    return block


def from_behind(value, axis, by):
    peers = lax.axis_size(axis)
    pairs = [(i, i + by) for i in range(peers) if 0 <= i + by < peers]
    return lax.ppermute(value, axis, pairs)


def neighbour_sum(center, rows_source):
    columns = jnp.pad(center, ((0, 0), (1, 1), (0, 0)))
    return rows_source[2:] + rows_source[:-2] + columns[:, 2:] + columns[:, :-2]


def operator_core(center, rows_source, section):
    return (
        0.8 * (section[:, :, None] * center + 0.25 * neighbour_sum(center, rows_source))
        - 0.2 * center
    )


def inner_modes(left, right):
    return jnp.einsum("rcm,rcn->mn", left, right, precision=lax.Precision.HIGHEST)


def apply_edge(vectors, section):
    padded = padded_2(vectors, (("rows", 0),), 1)
    return operator_core(vectors, padded, section)


def body(start_modes, contrast, rotations, ordering):
    subspace = start_modes[0]
    section = contrast[0]
    turnings = rotations[0]
    sequence = ordering[0]
    rows_here = subspace.shape[0]
    columns = subspace.shape[1]
    nmodes = subspace.shape[2]
    tiles = lax.axis_size("rows")
    pixels = rows_here * tiles * columns
    for sweep in range(ITERS):
        before = subspace
        current = apply_edge(before, section)
        for degree_step in range(2, DEGREE + 1):
            following = 2.0 * apply_edge(current, section) - before
            before, current = (current, following)
        gram_sum = lax.psum(inner_modes(current, current), "rows") / pixels
        factor_low = jnp.linalg.cholesky(gram_sum)
        mixing = lax.linalg.triangular_solve(
            factor_low, turnings[sweep], left_side=True, lower=True, transpose_a=True
        )
        picker = (sequence[sweep][None, :] == jnp.arange(nmodes, dtype=jnp.int32)[:, None]).astype(
            jnp.float32
        )
        mixing = jnp.dot(mixing, picker, precision=lax.Precision.HIGHEST)
        subspace = jnp.einsum("rcm,mn->rcn", current, mixing, precision=lax.Precision.HIGHEST)
    earlier = from_behind(subspace, "cuts", 1)
    earlier = jnp.where(lax.axis_index("cuts") == 0, start_modes[0], earlier)
    applied = apply_edge(subspace, section)
    coupling_term = inner_modes(earlier, subspace)
    rayleigh_term = inner_modes(subspace, applied)
    share_rows = nmodes // tiles
    coupling_sum, rayleigh_sum = lax.psum((coupling_term, rayleigh_term), "rows")
    coupling_part = lax.dynamic_slice_in_dim(
        coupling_sum, lax.axis_index("rows") * share_rows, share_rows, 0
    )
    rayleigh_part = lax.dynamic_slice_in_dim(
        rayleigh_sum, lax.axis_index("rows") * share_rows, share_rows, 0
    )
    return (subspace[None], (coupling_part / pixels)[None], (rayleigh_part / pixels)[None])


def solution(mesh):
    placed = (
        P("cuts", "rows", None, None),
        P("cuts", "rows", None),
        P("cuts", None, None, None),
        P("cuts", None, None),
    )
    return jax.shard_map(
        body,
        mesh=mesh,
        in_specs=placed,
        out_specs=(P("cuts", "rows", None, None), P("cuts", "rows", None), P("cuts", "rows", None)),
        check_vma=False,
    )
```

profile of v0, /device:TPU:2, one launch (start us, length us, event | category | flops | bytes accessed | tf_op | source)
XLA Modules:
  0.0 658.3 jit_solution(1508440093911116403)
XLA Ops:
  8.4 1.3 collective-permute-start
  9.7 4.6 collective-permute-start.1
  14.2 4.1 collective-permute-done
  20.8 1.3 collective-permute-start.2
  22.1 5.0 collective-permute-start.3
  27.1 3.2 collective-permute-done.2
  32.1 1.3 collective-permute-start.4
  33.4 5.0 collective-permute-start.5
  38.4 2.4 collective-permute-done.4
  40.8 1.5 collective-permute-done.5
  43.5 1.3 collective-permute-start.6
  44.8 5.0 collective-permute-start.7
  49.8 2.4 collective-permute-done.6
  52.2 1.5 collective-permute-done.7
  54.2 2.5 convolution_bitcast_fusion.5
  57.0 164.5 %all-reduce.14.cloned.1.call-done = f32[128,128]{0,1:T(8,128)} async-done(((f32[128,128]{0,1:T(8,128)}), f32[128,128]{0,1:T(8,128)}) %all-reduce.14.cloned.1.call-update) | async-done | bytes 65552 | tf_op jit(solution)/shard_map/psum | solution.py:66
  223.3 11.7 %cholesky.44 = f32[128,128]{1,0:T(8,128)S(1)} custom-call(f32[128,128]{1,0:T(8,128)S(1)} %fusion.98), custom_call_target="Cholesky" | custom-call | tf_op jit(solution)/shard_map/jit(cholesky)/cholesky | solution.py:67
  236.4 9.8 %custom-call.6 = f32[1,128,128]{1,2,0:T(8,128)S(1)} custom-call(f32[1,128,128]{2,1,0:T(8,128)S(1)} %fusion.89), custom_call_target="InvertDiagBlocksLowerTriangular" | custom-call | tf_op jit(solution)/shard_map/triangular_solve/custom-call.0 | solution.py:68
  247.6 1.3 collective-permute-start.8
  248.9 4.6 collective-permute-start.9
  253.5 2.4 collective-permute-done.8
  255.9 1.5 collective-permute-done.9
  257.9 1.3 collective-permute-start.10
  259.2 5.0 collective-permute-start.11
  264.3 2.4 collective-permute-done.10
  266.6 1.7 collective-permute-done.11
  269.0 1.3 collective-permute-start.12
  270.3 5.0 collective-permute-start.13
  275.3 2.8 collective-permute-done.12
  278.1 1.7 collective-permute-done.13
  279.8 1.3 fusion.27
  281.1 1.3 collective-permute-start.14
  282.4 5.3 collective-permute-start.15
  287.8 2.2 collective-permute-done.14
  290.0 1.5 collective-permute-done.15
  292.0 2.5 convolution_bitcast_fusion.3
  294.5 157.7 %all-reduce.16.cloned.1.call-done = f32[128,128]{0,1:T(8,128)} async-done(((f32[128,128]{0,1:T(8,128)}), f32[128,128]{0,1:T(8,128)}) %all-reduce.16.cloned.1.call-update) | async-done | bytes 65552 | tf_op jit(solution)/shard_map/psum | solution.py:66
  454.1 11.7 %cholesky.55 = f32[128,128]{1,0:T(8,128)S(1)} custom-call(f32[128,128]{1,0:T(8,128)S(1)} %fusion.94), custom_call_target="Cholesky" | custom-call | tf_op jit(solution)/shard_map/jit(cholesky)/cholesky | solution.py:67
  467.1 9.8 %custom-call.7 = f32[1,128,128]{1,2,0:T(8,128)S(1)} custom-call(f32[1,128,128]{2,1,0:T(8,128)S(1)} %fusion.90), custom_call_target="InvertDiagBlocksLowerTriangular" | custom-call | tf_op jit(solution)/shard_map/triangular_solve/custom-call.0 | solution.py:68
  478.3 1.9 collective-permute-start.16
  481.0 1.3 collective-permute-start.17
  482.3 5.3 collective-permute-start.18
  487.5 4.3 collective-permute-done.17
  491.8 1.4 collective-permute-done.18
  493.2 4.0 convolution_bitcast_fusion
  497.2 2.5 convolution_bitcast_fusion.1
  499.7 150.8 %all-reduce.18.cloned.1.call-done = (f32[128,128]{1,0:T(8,128)}, f32[128,128]{1,0:T(8,128)}) async-done(((f32[128,128]{1,0:T(8,128)}, f32[128,128]{1,0:T(8,128)}), (f32[128,128]{1,0:T(8,128)}, f32[128,128]{1,0:T(8,128)})) %all-reduce.18.cloned.1.call-update) | async-done | bytes 131088 | tf_op jit(solution)/shard_map/psum | solution.py:82
  650.5 1.3 multiply_bitcast_fusion
  (54 shorter events, 19.0 us)
Async XLA Ops:
  7.2 12.3 %copy-start = (f32[1,4,512,128]{3,2,1,0:T(8,128)S(1)}, f32[1,4,512,128]{3,2,1,0:T(8,128)}, u32[]{:S(2)}) copy-start(f32[1,4,512,128]{3,2,1,0:T(8,128)} %param.7) | copy-start | bytes 3145732
  7.2 214.3 %all-reduce.14.cloned.1.call-start = ((), (), s32[]{:S(2)}) async-start(), calls=%async_computation | async-start | bytes 131072 | tf_op jit(solution)/shard_map/psum | solution.py:66
  8.4 9.9 %collective-permute-start = (f32[1,512,128]{2,1,0:T(8,128)S(1)}, f32[1,512,128]{2,1,0:T(8,128)S(1)}, u32[]{:S(2)}, u32[]{:S(2)}) collective-permute-start(f32[1,512,128]{2,1,0:T(8,128)S(1)} %get-tuple-element.23), channel_id=1, source_target_pairs={{1,0},{2,1},{3,2},{4,3},{5,4},{6,5},{7,6},{8,7},{9,8},{10,9},{11,1... | collective-permute-start | bytes 786440 | tf_op jit(solution)/shard_map/ppermute | solution.py:18
  9.7 9.8 %collective-permute-start.1 = (f32[1,512,128]{2,1,0:T(8,128)S(1)}, f32[1,512,128]{2,1,0:T(8,128)S(1)}, u32[]{:S(2)}, u32[]{:S(2)}) collective-permute-start(f32[1,512,128]{2,1,0:T(8,128)S(1)} %get-tuple-element.24), channel_id=1, source_target_pairs={{0,1},{1,2},{2,3},{3,4},{4,5},{5,6},{6,7},{7,8},{8,9},{9,10},{10,1... | collective-permute-start | bytes 786440 | tf_op jit(solution)/shard_map/ppermute | solution.py:15
  20.7 10.7 %copy-start.2 = (f32[1,4,512]{2,1,0:T(4,128)S(1)}, f32[1,4,512]{2,1,0:T(4,128)}, u32[]{:S(2)}) copy-start(f32[1,4,512]{2,1,0:T(4,128)} %param.8) | copy-start | bytes 24580
  20.8 9.5 %collective-permute-start.2 = (f32[1,512,128]{2,1,0:T(8,128)S(1)}, f32[1,512,128]{2,1,0:T(8,128)S(1)}, u32[]{:S(2)}, u32[]{:S(2)}) collective-permute-start(f32[1,512,128]{2,1,0:T(8,128)S(1)} %get-tuple-element.21), channel_id=1, source_target_pairs={{1,0},{2,1},{3,2},{4,3},{5,4},{6,5},{7,6},{8,7},{9,8},{10,9},{11,1... | collective-permute-start | bytes 786440 | tf_op jit(solution)/shard_map/ppermute | solution.py:18
  22.1 9.4 %collective-permute-start.3 = (f32[1,512,128]{2,1,0:T(8,128)S(1)}, f32[1,512,128]{2,1,0:T(8,128)S(1)}, u32[]{:S(2)}, u32[]{:S(2)}) collective-permute-start(f32[1,512,128]{2,1,0:T(8,128)S(1)} %get-tuple-element.22), channel_id=1, source_target_pairs={{0,1},{1,2},{2,3},{3,4},{4,5},{5,6},{6,7},{7,8},{8,9},{9,10},{10,1... | collective-permute-start | bytes 786440 | tf_op jit(solution)/shard_map/ppermute | solution.py:15
  32.1 8.7 %collective-permute-start.4 = (f32[1,512,128]{2,1,0:T(8,128)S(1)}, f32[1,512,128]{2,1,0:T(8,128)S(1)}, u32[]{:S(2)}, u32[]{:S(2)}) collective-permute-start(f32[1,512,128]{2,1,0:T(8,128)S(1)} %get-tuple-element.19), channel_id=1, source_target_pairs={{1,0},{2,1},{3,2},{4,3},{5,4},{6,5},{7,6},{8,7},{9,8},{10,9},{11,1... | collective-permute-start | bytes 786440 | tf_op jit(solution)/shard_map/ppermute | solution.py:18
  33.4 8.9 %collective-permute-start.5 = (f32[1,512,128]{2,1,0:T(8,128)S(1)}, f32[1,512,128]{2,1,0:T(8,128)S(1)}, u32[]{:S(2)}, u32[]{:S(2)}) collective-permute-start(f32[1,512,128]{2,1,0:T(8,128)S(1)} %get-tuple-element.20), channel_id=1, source_target_pairs={{0,1},{1,2},{2,3},{3,4},{4,5},{5,6},{6,7},{7,8},{8,9},{9,10},{10,1... | collective-permute-start | bytes 786440 | tf_op jit(solution)/shard_map/ppermute | solution.py:15
  43.5 8.7 %collective-permute-start.6 = (f32[1,512,128]{2,1,0:T(8,128)S(1)}, f32[1,512,128]{2,1,0:T(8,128)S(1)}, u32[]{:S(2)}, u32[]{:S(2)}) collective-permute-start(f32[1,512,128]{2,1,0:T(8,128)S(1)} %get-tuple-element.17), channel_id=1, source_target_pairs={{1,0},{2,1},{3,2},{4,3},{5,4},{6,5},{7,6},{8,7},{9,8},{10,9},{11,1... | collective-permute-start | bytes 786440 | tf_op jit(solution)/shard_map/ppermute | solution.py:18
  44.8 8.9 %collective-permute-start.7 = (f32[1,512,128]{2,1,0:T(8,128)S(1)}, f32[1,512,128]{2,1,0:T(8,128)S(1)}, u32[]{:S(2)}, u32[]{:S(2)}) collective-permute-start(f32[1,512,128]{2,1,0:T(8,128)S(1)} %get-tuple-element.18), channel_id=1, source_target_pairs={{0,1},{1,2},{2,3},{3,4},{4,5},{5,6},{6,7},{7,8},{8,9},{9,10},{10,1... | collective-permute-start | bytes 786440 | tf_op jit(solution)/shard_map/ppermute | solution.py:15
  54.2 2.8 copy-start.4
  54.2 191.9 %copy-start.3 = (f32[1,2,128,128]{3,2,1,0:T(8,128)S(1)}, f32[1,2,128,128]{3,2,1,0:T(8,128)}, u32[]{:S(2)}) copy-start(f32[1,2,128,128]{3,2,1,0:T(8,128)} %param.9) | copy-start | bytes 393220
  56.8 395.5 %all-reduce.16.cloned.1.call-start = ((), (), s32[]{:S(2)}) async-start(), calls=%async_computation.1 | async-start | bytes 131072 | tf_op jit(solution)/shard_map/psum | solution.py:66
  247.6 8.3 %collective-permute-start.8 = (f32[1,512,128]{2,1,0:T(8,128)S(1)}, f32[1,512,128]{2,1,0:T(8,128)S(1)}, u32[]{:S(2)}, u32[]{:S(2)}) collective-permute-start(f32[1,512,128]{2,1,0:T(8,128)S(1)} %get-tuple-element.15), channel_id=1, source_target_pairs={{1,0},{2,1},{3,2},{4,3},{5,4},{6,5},{7,6},{8,7},{9,8},{10,9},{11,1... | collective-permute-start | bytes 786440 | tf_op jit(solution)/shard_map/ppermute | solution.py:18
  248.9 8.4 %collective-permute-start.9 = (f32[1,512,128]{2,1,0:T(8,128)S(1)}, f32[1,512,128]{2,1,0:T(8,128)S(1)}, u32[]{:S(2)}, u32[]{:S(2)}) collective-permute-start(f32[1,512,128]{2,1,0:T(8,128)S(1)} %get-tuple-element.16), channel_id=1, source_target_pairs={{0,1},{1,2},{2,3},{3,4},{4,5},{5,6},{6,7},{7,8},{8,9},{9,10},{10,1... | collective-permute-start | bytes 786440 | tf_op jit(solution)/shard_map/ppermute | solution.py:15
  257.9 8.7 %collective-permute-start.10 = (f32[1,512,128]{2,1,0:T(8,128)S(1)}, f32[1,512,128]{2,1,0:T(8,128)S(1)}, u32[]{:S(2)}, u32[]{:S(2)}) collective-permute-start(f32[1,512,128]{2,1,0:T(8,128)S(1)} %get-tuple-element.13), channel_id=1, source_target_pairs={{1,0},{2,1},{3,2},{4,3},{5,4},{6,5},{7,6},{8,7},{9,8},{10,9},{11,1... | collective-permute-start | bytes 786440 | tf_op jit(solution)/shard_map/ppermute | solution.py:18
  259.2 9.2 %collective-permute-start.11 = (f32[1,512,128]{2,1,0:T(8,128)S(1)}, f32[1,512,128]{2,1,0:T(8,128)S(1)}, u32[]{:S(2)}, u32[]{:S(2)}) collective-permute-start(f32[1,512,128]{2,1,0:T(8,128)S(1)} %get-tuple-element.14), channel_id=1, source_target_pairs={{0,1},{1,2},{2,3},{3,4},{4,5},{5,6},{6,7},{7,8},{8,9},{9,10},{10,1... | collective-permute-start | bytes 786440 | tf_op jit(solution)/shard_map/ppermute | solution.py:15
  269.0 9.1 %collective-permute-start.12 = (f32[1,512,128]{2,1,0:T(8,128)S(1)}, f32[1,512,128]{2,1,0:T(8,128)S(1)}, u32[]{:S(2)}, u32[]{:S(2)}) collective-permute-start(f32[1,512,128]{2,1,0:T(8,128)S(1)} %get-tuple-element.11), channel_id=1, source_target_pairs={{1,0},{2,1},{3,2},{4,3},{5,4},{6,5},{7,6},{8,7},{9,8},{10,9},{11,1... | collective-permute-start | bytes 786440 | tf_op jit(solution)/shard_map/ppermute | solution.py:18
  270.3 9.5 %collective-permute-start.13 = (f32[1,512,128]{2,1,0:T(8,128)S(1)}, f32[1,512,128]{2,1,0:T(8,128)S(1)}, u32[]{:S(2)}, u32[]{:S(2)}) collective-permute-start(f32[1,512,128]{2,1,0:T(8,128)S(1)} %get-tuple-element.12), channel_id=1, source_target_pairs={{0,1},{1,2},{2,3},{3,4},{4,5},{5,6},{6,7},{7,8},{8,9},{9,10},{10,1... | collective-permute-start | bytes 786440 | tf_op jit(solution)/shard_map/ppermute | solution.py:15
  281.1 8.8 %collective-permute-start.14 = (f32[1,512,128]{2,1,0:T(8,128)S(1)}, f32[1,512,128]{2,1,0:T(8,128)S(1)}, u32[]{:S(2)}, u32[]{:S(2)}) collective-permute-start(f32[1,512,128]{2,1,0:T(8,128)S(1)} %get-tuple-element.9), channel_id=1, source_target_pairs={{1,0},{2,1},{3,2},{4,3},{5,4},{6,5},{7,6},{8,7},{9,8},{10,9},{11,1... | collective-permute-start | bytes 786440 | tf_op jit(solution)/shard_map/ppermute | solution.py:18
  282.4 9.0 %collective-permute-start.15 = (f32[1,512,128]{2,1,0:T(8,128)S(1)}, f32[1,512,128]{2,1,0:T(8,128)S(1)}, u32[]{:S(2)}, u32[]{:S(2)}) collective-permute-start(f32[1,512,128]{2,1,0:T(8,128)S(1)} %get-tuple-element.10), channel_id=1, source_target_pairs={{0,1},{1,2},{2,3},{3,4},{4,5},{5,6},{6,7},{7,8},{8,9},{9,10},{10,1... | collective-permute-start | bytes 786440 | tf_op jit(solution)/shard_map/ppermute | solution.py:15
  294.5 356.0 %all-reduce.18.cloned.1.call-start = ((), (), s32[]{:S(2)}) async-start(), calls=%async_computation.2 | async-start | bytes 262144 | tf_op jit(solution)/shard_map/psum | solution.py:82
  478.3 18.9 %copy-start.1 = (f32[4,512,128]{2,1,0:T(8,128)}, f32[4,512,128]{2,1,0:T(8,128)S(1)}, u32[]{:S(2)}) copy-start(f32[4,512,128]{2,1,0:T(8,128)S(1)} %fusion.118) | copy-start | bytes 3145732
  478.3 18.9 %collective-permute-start.16 = (f32[4,512,128]{2,1,0:T(8,128)S(1)}, f32[4,512,128]{2,1,0:T(8,128)S(1)}, u32[]{:S(2)}, u32[]{:S(2)}) collective-permute-start(f32[4,512,128]{2,1,0:T(8,128)S(1)} %fusion.118), channel_id=1, source_target_pairs={{0,64},{64,128},{128,192},{192,256},{256,320},{320,384},{384,448},... | collective-permute-start | bytes 3145736 | tf_op jit(solution)/shard_map/ppermute | solution.py:26
  481.0 10.8 %collective-permute-start.17 = (f32[1,512,128]{2,1,0:T(8,128)}, f32[1,512,128]{2,1,0:T(8,128)}, u32[]{:S(2)}, u32[]{:S(2)}) collective-permute-start(f32[1,512,128]{2,1,0:T(8,128)} %get-tuple-element.7), channel_id=1, source_target_pairs={{1,0},{2,1},{3,2},{4,3},{5,4},{6,5},{7,6},{8,7},{9,8},{10,9},{11,1... | collective-permute-start | bytes 786440 | tf_op jit(solution)/shard_map/ppermute | solution.py:18
  482.3 10.9 %collective-permute-start.18 = (f32[1,512,128]{2,1,0:T(8,128)S(1)}, f32[1,512,128]{2,1,0:T(8,128)}, u32[]{:S(2)}, u32[]{:S(2)}) collective-permute-start(f32[1,512,128]{2,1,0:T(8,128)S(1)} %get-tuple-element.8), channel_id=1, source_target_pairs={{0,1},{1,2},{2,3},{3,4},{4,5},{5,6},{6,7},{7,8},{8,9},{9,10},{10,1... | collective-permute-start | bytes 786440 | tf_op jit(solution)/shard_map/ppermute | solution.py:15
Sparse Core Ops, SparseCore 0:
  56.9 164.5 all-reduce.13
  294.6 157.5 all-reduce.15
  499.8 150.6 all-reduce.17
where the time goes:
time: 659 us; the launch traced here: 658 us
  waiting for transfers between devices  512 us (78%)
  starting transfers between devices  58.7 us (9%)
  other arithmetic  56.7 us (9%)
  matrix products  14.2 us (2%)
  between operations  14.2 us (2%)
    psum x2, waiting for transfers between devices, body(): gram_sum = lax.psum(inner_modes(current, current), 'rows') / pixels  322 us
    psum x1, waiting for transfers between devices, body(): lax.psum((coupling_term, rayleigh_term), 'rows')  151 us
    ppermute x9, starting transfers between devices, padded_2(): lax.ppermute(lax.slice_in_dim(block, block.shape[dim] - width, None, axis...  44.9 us
    ppermute x9, waiting for transfers between devices, padded_2(): lax.ppermute(lax.slice_in_dim(block, 0, width, axis=dim), axis, backward)  26 us
    another operation x6, other arithmetic, body(): factor_low = jnp.linalg.cholesky(gram_sum)  24.8 us
    another operation x4, other arithmetic, body(): lax.linalg.triangular_solve(factor_low, turnings[sweep], left_side=True,...  20.9 us
  transfers between devices with their start and end apart: 22, of which 21 were waited for; matrix products, arithmetic and copies ran while one was open for 1% of the time, Pallas kernels for 0%

commit v1 on v0

--- a/solution.py
+++ b/solution.py
@@ -5,6 +5,12 @@
 
 DEGREE = 4
 ITERS = 2
+
+
+def summed_here(value, mesh_axis):
+    terms = lax.all_gather(value, mesh_axis, axis=0, tiled=False)
+    acc = terms.sum(axis=0)
+    return acc
 
 
 def padded_2(block, sides, width):
@@ -63,7 +69,7 @@
         for degree_step in range(2, DEGREE + 1):
             following = 2.0 * apply_edge(current, section) - before
             before, current = (current, following)
-        gram_sum = lax.psum(inner_modes(current, current), "rows") / pixels
+        gram_sum = summed_here(inner_modes(current, current), "rows") / pixels
         factor_low = jnp.linalg.cholesky(gram_sum)
         mixing = lax.linalg.triangular_solve(
             factor_low, turnings[sweep], left_side=True, lower=True, transpose_a=True

time: 659 us -> 539 us (0.82)
  waiting for transfers between devices: 512 us -> 391 us
    psum x2 -> x0, waiting for transfers between devices: 322 us -> none  [body(): gram_sum = lax.psum(inner_modes(current, current), 'rows') / pixels]
    all_gather x0 -> x2, waiting for transfers between devices: none -> 200 us  [summed_here(): terms = lax.all_gather(value, mesh_axis, axis=0, tiled=False)]
where the time goes in v1:
time: 539 us; the launch traced here: 538 us
  waiting for transfers between devices  391 us (73%)
  starting transfers between devices  58.6 us (11%)
  other arithmetic  58.3 us (11%)
  between operations  14.2 us (3%)
  matrix products  14 us (3%)
    all_gather x2, waiting for transfers between devices, summed_here(): terms = lax.all_gather(value, mesh_axis, axis=0, tiled=False)  200 us
    psum x1, waiting for transfers between devices, body(): lax.psum((coupling_term, rayleigh_term), 'rows')  152 us
    ppermute x9, starting transfers between devices, padded_2(): lax.ppermute(lax.slice_in_dim(block, block.shape[dim] - width, None, axis...  44.8 us
    ppermute x9, waiting for transfers between devices, padded_2(): lax.ppermute(lax.slice_in_dim(block, 0, width, axis=dim), axis, backward)  25.7 us
    another operation x6, other arithmetic, body(): factor_low = jnp.linalg.cholesky(gram_sum)  24.8 us
    another operation x4, other arithmetic, body(): lax.linalg.triangular_solve(factor_low, turnings[sweep], left_side=True,...  20.9 us
    ppermute x9, waiting for transfers between devices, padded_2(): lax.ppermute(lax.slice_in_dim(block, block.shape[dim] - width, None, axis...  12.5 us
    ppermute x9, starting transfers between devices, padded_2(): lax.ppermute(lax.slice_in_dim(block, 0, width, axis=dim), axis, backward)  11.6 us
  transfers between devices with their start and end apart: 22, of which 21 were waited for; matrix products, arithmetic and copies ran while one was open for 1% of the time, Pallas kernels for 0%

profile of v1, /device:TPU:2, one launch (start us, length us, event | category | flops | bytes accessed | tf_op | source)
XLA Modules:
  0.0 538.1 jit_solution(4606689985389857948)
XLA Ops:
  8.4 1.3 collective-permute-start
  9.7 4.6 collective-permute-start.1
  14.2 4.1 collective-permute-done
  19.5 1.3 fusion.77
  20.8 1.3 collective-permute-start.2
  22.1 5.0 collective-permute-start.3
  27.2 3.2 collective-permute-done.2
  32.1 1.3 collective-permute-start.4
  33.4 5.0 collective-permute-start.5
  38.4 2.4 collective-permute-done.4
  40.8 1.5 collective-permute-done.5
  43.6 1.3 collective-permute-start.6
  44.9 5.0 collective-permute-start.7
  49.9 2.4 collective-permute-done.6
  52.3 1.5 collective-permute-done.7
  54.3 2.5 convolution_bitcast_fusion.5
  57.1 102.7 %all-gather.5.cloned.1.call-done = f32[8192,128]{1,0:T(8,128)} async-done(((f32[128,128]{1,0:T(8,128)}), f32[8192,128]{1,0:T(8,128)}) %all-gather.5.cloned.1.call-update) | async-done | bytes 4194320 | tf_op jit(solution)/shard_map/all_gather | solution.py:11
  159.7 2.4 reduce_sum.18
  162.4 11.7 %cholesky.44 = f32[128,128]{1,0:T(8,128)S(1)} custom-call(f32[128,128]{1,0:T(8,128)S(1)} %fusion.98), custom_call_target="Cholesky" | custom-call | tf_op jit(solution)/shard_map/jit(cholesky)/cholesky | solution.py:73
  175.4 9.8 %custom-call.6 = f32[1,128,128]{1,2,0:T(8,128)S(1)} custom-call(f32[1,128,128]{2,1,0:T(8,128)S(1)} %fusion.89), custom_call_target="InvertDiagBlocksLowerTriangular" | custom-call | tf_op jit(solution)/shard_map/triangular_solve/custom-call.0 | solution.py:74
  186.7 1.3 collective-permute-start.8
  188.0 4.6 collective-permute-start.9
  192.6 2.4 collective-permute-done.8
  195.0 1.5 collective-permute-done.9
  197.0 1.3 collective-permute-start.10
  198.3 5.0 collective-permute-start.11
  203.3 2.4 collective-permute-done.10
  205.7 1.5 collective-permute-done.11
  207.8 1.3 collective-permute-start.12
  209.1 5.0 collective-permute-start.13
  214.1 2.4 collective-permute-done.12
  216.5 1.5 collective-permute-done.13
  219.2 1.3 collective-permute-start.14
  220.5 5.3 collective-permute-start.15
  225.8 2.2 collective-permute-done.14
  228.0 1.5 collective-permute-done.15
  230.0 2.5 convolution_bitcast_fusion.3
  232.5 97.8 %all-gather.7.cloned.1.call-done = f32[8192,128]{1,0:T(8,128)} async-done(((f32[128,128]{1,0:T(8,128)}), f32[8192,128]{1,0:T(8,128)}) %all-gather.7.cloned.1.call-update) | async-done | bytes 4194320 | tf_op jit(solution)/shard_map/all_gather | solution.py:11
  330.3 2.4 reduce_sum.19
  332.9 11.7 %cholesky.55 = f32[128,128]{1,0:T(8,128)S(1)} custom-call(f32[128,128]{1,0:T(8,128)S(1)} %fusion.94), custom_call_target="Cholesky" | custom-call | tf_op jit(solution)/shard_map/jit(cholesky)/cholesky | solution.py:73
  346.0 9.8 %custom-call.7 = f32[1,128,128]{1,2,0:T(8,128)S(1)} custom-call(f32[1,128,128]{2,1,0:T(8,128)S(1)} %fusion.90), custom_call_target="InvertDiagBlocksLowerTriangular" | custom-call | tf_op jit(solution)/shard_map/triangular_solve/custom-call.0 | solution.py:74
  357.2 1.9 collective-permute-start.16
  361.1 5.3 collective-permute-start.18
  366.4 4.3 collective-permute-done.17
  370.7 1.4 collective-permute-done.18
  372.0 3.9 convolution_bitcast_fusion
  375.9 2.5 convolution_bitcast_fusion.1
  378.4 151.9 %all-reduce.12.cloned.1.call-done = (f32[128,128]{1,0:T(8,128)}, f32[128,128]{1,0:T(8,128)}) async-done(((f32[128,128]{1,0:T(8,128)}, f32[128,128]{1,0:T(8,128)}), (f32[128,128]{1,0:T(8,128)}, f32[128,128]{1,0:T(8,128)})) %all-reduce.12.cloned.1.call-update) | async-done | bytes 131088 | tf_op jit(solution)/shard_map/psum | solution.py:88
  (58 shorter events, 18.3 us)
Async XLA Ops:
  7.2 12.3 %copy-start = (f32[1,4,512,128]{3,2,1,0:T(8,128)S(1)}, f32[1,4,512,128]{3,2,1,0:T(8,128)}, u32[]{:S(2)}) copy-start(f32[1,4,512,128]{3,2,1,0:T(8,128)} %param.7) | copy-start | bytes 3145732
  7.2 152.5 %all-gather.5.cloned.1.call-start = ((), (), s32[]{:S(2)}) async-start(), calls=%async_computation | async-start | bytes 4259840 | tf_op jit(solution)/shard_map/all_gather | solution.py:11
  8.4 9.9 %collective-permute-start = (f32[1,512,128]{2,1,0:T(8,128)S(1)}, f32[1,512,128]{2,1,0:T(8,128)S(1)}, u32[]{:S(2)}, u32[]{:S(2)}) collective-permute-start(f32[1,512,128]{2,1,0:T(8,128)S(1)} %get-tuple-element.23), channel_id=1, source_target_pairs={{1,0},{2,1},{3,2},{4,3},{5,4},{6,5},{7,6},{8,7},{9,8},{10,9},{11,1... | collective-permute-start | bytes 786440 | tf_op jit(solution)/shard_map/ppermute | solution.py:24
  9.7 9.8 %collective-permute-start.1 = (f32[1,512,128]{2,1,0:T(8,128)S(1)}, f32[1,512,128]{2,1,0:T(8,128)S(1)}, u32[]{:S(2)}, u32[]{:S(2)}) collective-permute-start(f32[1,512,128]{2,1,0:T(8,128)S(1)} %get-tuple-element.24), channel_id=1, source_target_pairs={{0,1},{1,2},{2,3},{3,4},{4,5},{5,6},{6,7},{7,8},{8,9},{9,10},{10,1... | collective-permute-start | bytes 786440 | tf_op jit(solution)/shard_map/ppermute | solution.py:21
  19.5 12.0 %copy-start.2 = (f32[1,4,512]{2,1,0:T(4,128)S(1)}, f32[1,4,512]{2,1,0:T(4,128)}, u32[]{:S(2)}) copy-start(f32[1,4,512]{2,1,0:T(4,128)} %param.8) | copy-start | bytes 24580
  20.8 9.5 %collective-permute-start.2 = (f32[1,512,128]{2,1,0:T(8,128)S(1)}, f32[1,512,128]{2,1,0:T(8,128)S(1)}, u32[]{:S(2)}, u32[]{:S(2)}) collective-permute-start(f32[1,512,128]{2,1,0:T(8,128)S(1)} %get-tuple-element.21), channel_id=1, source_target_pairs={{1,0},{2,1},{3,2},{4,3},{5,4},{6,5},{7,6},{8,7},{9,8},{10,9},{11,1... | collective-permute-start | bytes 786440 | tf_op jit(solution)/shard_map/ppermute | solution.py:24
  22.1 9.4 %collective-permute-start.3 = (f32[1,512,128]{2,1,0:T(8,128)S(1)}, f32[1,512,128]{2,1,0:T(8,128)S(1)}, u32[]{:S(2)}, u32[]{:S(2)}) collective-permute-start(f32[1,512,128]{2,1,0:T(8,128)S(1)} %get-tuple-element.22), channel_id=1, source_target_pairs={{0,1},{1,2},{2,3},{3,4},{4,5},{5,6},{6,7},{7,8},{8,9},{9,10},{10,1... | collective-permute-start | bytes 786440 | tf_op jit(solution)/shard_map/ppermute | solution.py:21
  32.1 8.7 %collective-permute-start.4 = (f32[1,512,128]{2,1,0:T(8,128)S(1)}, f32[1,512,128]{2,1,0:T(8,128)S(1)}, u32[]{:S(2)}, u32[]{:S(2)}) collective-permute-start(f32[1,512,128]{2,1,0:T(8,128)S(1)} %get-tuple-element.19), channel_id=1, source_target_pairs={{1,0},{2,1},{3,2},{4,3},{5,4},{6,5},{7,6},{8,7},{9,8},{10,9},{11,1... | collective-permute-start | bytes 786440 | tf_op jit(solution)/shard_map/ppermute | solution.py:24
  33.4 8.9 %collective-permute-start.5 = (f32[1,512,128]{2,1,0:T(8,128)S(1)}, f32[1,512,128]{2,1,0:T(8,128)S(1)}, u32[]{:S(2)}, u32[]{:S(2)}) collective-permute-start(f32[1,512,128]{2,1,0:T(8,128)S(1)} %get-tuple-element.20), channel_id=1, source_target_pairs={{0,1},{1,2},{2,3},{3,4},{4,5},{5,6},{6,7},{7,8},{8,9},{9,10},{10,1... | collective-permute-start | bytes 786440 | tf_op jit(solution)/shard_map/ppermute | solution.py:21
  43.6 8.7 %collective-permute-start.6 = (f32[1,512,128]{2,1,0:T(8,128)S(1)}, f32[1,512,128]{2,1,0:T(8,128)S(1)}, u32[]{:S(2)}, u32[]{:S(2)}) collective-permute-start(f32[1,512,128]{2,1,0:T(8,128)S(1)} %get-tuple-element.17), channel_id=1, source_target_pairs={{1,0},{2,1},{3,2},{4,3},{5,4},{6,5},{7,6},{8,7},{9,8},{10,9},{11,1... | collective-permute-start | bytes 786440 | tf_op jit(solution)/shard_map/ppermute | solution.py:24
  44.9 8.9 %collective-permute-start.7 = (f32[1,512,128]{2,1,0:T(8,128)S(1)}, f32[1,512,128]{2,1,0:T(8,128)S(1)}, u32[]{:S(2)}, u32[]{:S(2)}) collective-permute-start(f32[1,512,128]{2,1,0:T(8,128)S(1)} %get-tuple-element.18), channel_id=1, source_target_pairs={{0,1},{1,2},{2,3},{3,4},{4,5},{5,6},{6,7},{7,8},{8,9},{9,10},{10,1... | collective-permute-start | bytes 786440 | tf_op jit(solution)/shard_map/ppermute | solution.py:21
  54.3 2.7 copy-start.4
  56.8 273.5 %all-gather.7.cloned.1.call-start = ((), (), s32[]{:S(2)}) async-start(), calls=%async_computation.1 | async-start | bytes 4259840 | tf_op jit(solution)/shard_map/all_gather | solution.py:11
  159.7 25.5 %copy-start.3 = (f32[1,2,128,128]{3,2,1,0:T(8,128)S(1)}, f32[1,2,128,128]{3,2,1,0:T(8,128)}, u32[]{:S(2)}) copy-start(f32[1,2,128,128]{3,2,1,0:T(8,128)} %param.9) | copy-start | bytes 393220
  186.7 8.3 %collective-permute-start.8 = (f32[1,512,128]{2,1,0:T(8,128)S(1)}, f32[1,512,128]{2,1,0:T(8,128)S(1)}, u32[]{:S(2)}, u32[]{:S(2)}) collective-permute-start(f32[1,512,128]{2,1,0:T(8,128)S(1)} %get-tuple-element.15), channel_id=1, source_target_pairs={{1,0},{2,1},{3,2},{4,3},{5,4},{6,5},{7,6},{8,7},{9,8},{10,9},{11,1... | collective-permute-start | bytes 786440 | tf_op jit(solution)/shard_map/ppermute | solution.py:24
  188.0 8.4 %collective-permute-start.9 = (f32[1,512,128]{2,1,0:T(8,128)S(1)}, f32[1,512,128]{2,1,0:T(8,128)S(1)}, u32[]{:S(2)}, u32[]{:S(2)}) collective-permute-start(f32[1,512,128]{2,1,0:T(8,128)S(1)} %get-tuple-element.16), channel_id=1, source_target_pairs={{0,1},{1,2},{2,3},{3,4},{4,5},{5,6},{6,7},{7,8},{8,9},{9,10},{10,1... | collective-permute-start | bytes 786440 | tf_op jit(solution)/shard_map/ppermute | solution.py:21
  197.0 8.7 %collective-permute-start.10 = (f32[1,512,128]{2,1,0:T(8,128)S(1)}, f32[1,512,128]{2,1,0:T(8,128)S(1)}, u32[]{:S(2)}, u32[]{:S(2)}) collective-permute-start(f32[1,512,128]{2,1,0:T(8,128)S(1)} %get-tuple-element.13), channel_id=1, source_target_pairs={{1,0},{2,1},{3,2},{4,3},{5,4},{6,5},{7,6},{8,7},{9,8},{10,9},{11,1... | collective-permute-start | bytes 786440 | tf_op jit(solution)/shard_map/ppermute | solution.py:24
  198.3 8.9 %collective-permute-start.11 = (f32[1,512,128]{2,1,0:T(8,128)S(1)}, f32[1,512,128]{2,1,0:T(8,128)S(1)}, u32[]{:S(2)}, u32[]{:S(2)}) collective-permute-start(f32[1,512,128]{2,1,0:T(8,128)S(1)} %get-tuple-element.14), channel_id=1, source_target_pairs={{0,1},{1,2},{2,3},{3,4},{4,5},{5,6},{6,7},{7,8},{8,9},{9,10},{10,1... | collective-permute-start | bytes 786440 | tf_op jit(solution)/shard_map/ppermute | solution.py:21
  207.8 8.7 %collective-permute-start.12 = (f32[1,512,128]{2,1,0:T(8,128)S(1)}, f32[1,512,128]{2,1,0:T(8,128)S(1)}, u32[]{:S(2)}, u32[]{:S(2)}) collective-permute-start(f32[1,512,128]{2,1,0:T(8,128)S(1)} %get-tuple-element.11), channel_id=1, source_target_pairs={{1,0},{2,1},{3,2},{4,3},{5,4},{6,5},{7,6},{8,7},{9,8},{10,9},{11,1... | collective-permute-start | bytes 786440 | tf_op jit(solution)/shard_map/ppermute | solution.py:24
  209.1 8.9 %collective-permute-start.13 = (f32[1,512,128]{2,1,0:T(8,128)S(1)}, f32[1,512,128]{2,1,0:T(8,128)S(1)}, u32[]{:S(2)}, u32[]{:S(2)}) collective-permute-start(f32[1,512,128]{2,1,0:T(8,128)S(1)} %get-tuple-element.12), channel_id=1, source_target_pairs={{0,1},{1,2},{2,3},{3,4},{4,5},{5,6},{6,7},{7,8},{8,9},{9,10},{10,1... | collective-permute-start | bytes 786440 | tf_op jit(solution)/shard_map/ppermute | solution.py:21
  219.2 8.7 %collective-permute-start.14 = (f32[1,512,128]{2,1,0:T(8,128)S(1)}, f32[1,512,128]{2,1,0:T(8,128)S(1)}, u32[]{:S(2)}, u32[]{:S(2)}) collective-permute-start(f32[1,512,128]{2,1,0:T(8,128)S(1)} %get-tuple-element.9), channel_id=1, source_target_pairs={{1,0},{2,1},{3,2},{4,3},{5,4},{6,5},{7,6},{8,7},{9,8},{10,9},{11,1... | collective-permute-start | bytes 786440 | tf_op jit(solution)/shard_map/ppermute | solution.py:24
  220.5 8.9 %collective-permute-start.15 = (f32[1,512,128]{2,1,0:T(8,128)S(1)}, f32[1,512,128]{2,1,0:T(8,128)S(1)}, u32[]{:S(2)}, u32[]{:S(2)}) collective-permute-start(f32[1,512,128]{2,1,0:T(8,128)S(1)} %get-tuple-element.10), channel_id=1, source_target_pairs={{0,1},{1,2},{2,3},{3,4},{4,5},{5,6},{6,7},{7,8},{8,9},{9,10},{10,1... | collective-permute-start | bytes 786440 | tf_op jit(solution)/shard_map/ppermute | solution.py:21
  232.5 297.9 %all-reduce.12.cloned.1.call-start = ((), (), s32[]{:S(2)}) async-start(), calls=%async_computation.2 | async-start | bytes 262144 | tf_op jit(solution)/shard_map/psum | solution.py:88
  357.2 18.8 %copy-start.1 = (f32[4,512,128]{2,1,0:T(8,128)}, f32[4,512,128]{2,1,0:T(8,128)S(1)}, u32[]{:S(2)}) copy-start(f32[4,512,128]{2,1,0:T(8,128)S(1)} %fusion.118) | copy-start | bytes 3145732
  357.2 18.8 %collective-permute-start.16 = (f32[4,512,128]{2,1,0:T(8,128)S(1)}, f32[4,512,128]{2,1,0:T(8,128)S(1)}, u32[]{:S(2)}, u32[]{:S(2)}) collective-permute-start(f32[4,512,128]{2,1,0:T(8,128)S(1)} %fusion.118), channel_id=1, source_target_pairs={{0,64},{64,128},{128,192},{192,256},{256,320},{320,384},{384,448},... | collective-permute-start | bytes 3145736 | tf_op jit(solution)/shard_map/ppermute | solution.py:32
  359.8 10.8 %collective-permute-start.17 = (f32[1,512,128]{2,1,0:T(8,128)}, f32[1,512,128]{2,1,0:T(8,128)}, u32[]{:S(2)}, u32[]{:S(2)}) collective-permute-start(f32[1,512,128]{2,1,0:T(8,128)} %get-tuple-element.7), channel_id=1, source_target_pairs={{1,0},{2,1},{3,2},{4,3},{5,4},{6,5},{7,6},{8,7},{9,8},{10,9},{11,1... | collective-permute-start | bytes 786440 | tf_op jit(solution)/shard_map/ppermute | solution.py:24
  361.1 10.9 %collective-permute-start.18 = (f32[1,512,128]{2,1,0:T(8,128)S(1)}, f32[1,512,128]{2,1,0:T(8,128)}, u32[]{:S(2)}, u32[]{:S(2)}) collective-permute-start(f32[1,512,128]{2,1,0:T(8,128)S(1)} %get-tuple-element.8), channel_id=1, source_target_pairs={{0,1},{1,2},{2,3},{3,4},{4,5},{5,6},{6,7},{7,8},{8,9},{9,10},{10,1... | collective-permute-start | bytes 786440 | tf_op jit(solution)/shard_map/ppermute | solution.py:21
Sparse Core Ops, SparseCore 0:
  56.9 102.7 all-gather.4
  232.6 97.6 all-gather.6
  378.5 151.7 all-reduce.11
